TPU v7x, 256 devices: a whole 4x4x8 slice. The times are simulated.
256 devices in a mesh: chol: 16 (over x_lo, y, core), orb: 16 (over x_hi, z).
Axes of the slice: x: 4 (x_hi: 2, x_lo: 2; x = x_hi * 2 + x_lo), y: 4, z: 8, core: 2. Of those that a mesh axis runs over, the one named last changes fastest.
Arguments:
- phi_walkers: bfloat16 [16, 200, 1024], P('chol', None, 'orb'), may hold values from -6 to 6
- theta_half: bfloat16 [16, 200, 1024], P(None, None, 'orb'), may hold values from -0.5 to 0.5
- chol_vectors: bfloat16 [1024, 1024, 1024], P('chol', 'orb'), may hold values from -0.0034179688 to 0.0034179688
- chol_rotated: bfloat16 [1024, 200, 1024], P('chol', None, 'orb'), may hold values from -0.4375 to 0.4375
- hcore_rotated: bfloat16 [200, 1024], P(None, 'orb'), may hold values from -0.5 to 0.5
- aux_fields: float32 [16, 1024], P(None, 'chol'), may hold values from -6 to 6
Outputs:
- walkers_out: bfloat16 [16, 200, 1024], P('chol', None, 'orb')
- energy: float32 [16], replicated
All inputs are finite; a program needn't handle non-finite values.
Results may differ from a plain program's by a relative error of at most 0.013.
Values may be sent and summed in bfloat16 or wider, within the bound.
A program may use at most 128 MiB of HBM per device.

v0:
```python
import jax
import jax.numpy as jnp
from jax import lax
from jax.sharding import PartitionSpec as P

ORDER = 4


def body(phi_walkers, theta_half, chol_vectors, chol_rotated, hcore_rotated, aux_fields):
    walk_local = phi_walkers.shape[0]
    chol_local = chol_vectors.shape[0]
    rows_local = chol_vectors.shape[1]
    orbitals = chol_vectors.shape[2]
    per_group = chol_local // lax.axis_size("orb")
    walkers_all = theta_half.shape[0]
    flat_theta = theta_half.reshape(walkers_all, -1)
    bias_part = jnp.dot(
        flat_theta, chol_rotated.reshape(chol_local, -1).T, preferred_element_type=jnp.float32
    )
    one_part = jnp.dot(flat_theta, hcore_rotated.reshape(-1), preferred_element_type=jnp.float32)
    force_bias, one_body = lax.psum((bias_part, one_part), "orb")
    shifted = (aux_fields - force_bias).astype(jnp.bfloat16)
    flat_chol = chol_vectors.reshape(chol_local, -1)
    partial_operator = jnp.dot(shifted, flat_chol, preferred_element_type=jnp.float32)
    summed_operator = lax.psum(partial_operator, "chol")
    own_operator = lax.dynamic_slice_in_dim(
        summed_operator, lax.axis_index("chol") * walk_local, walk_local, 0
    )
    operator = own_operator.reshape(walk_local, rows_local, orbitals).astype(jnp.bfloat16)
    current = phi_walkers
    accumulated = phi_walkers.astype(jnp.float32)
    for degree in range(1, ORDER + 1):
        product = jnp.einsum(
            "wen,wpn->wep",
            lax.all_gather(current, "orb", axis=2, tiled=True),
            operator,
            preferred_element_type=jnp.float32,
        )
        current = (product / degree).astype(jnp.bfloat16)
        accumulated = accumulated + current.astype(jnp.float32)
    walkers_out = accumulated.astype(jnp.bfloat16)
    rotated_mine = lax.all_to_all(chol_rotated, "orb", split_axis=0, concat_axis=2, tiled=True)
    theta_full = lax.all_gather(theta_half, "orb", axis=2, tiled=True)

    def vector_pairs(single):
        pair_matrix = jnp.einsum(
            "en,wfn->wef", single, theta_full, preferred_element_type=jnp.float32
        )
        return jnp.einsum("wef,wfe->w", pair_matrix, pair_matrix)

    pairs_sum = jnp.sum(lax.map(vector_pairs, rotated_mine), axis=0)
    own_bias = lax.dynamic_slice_in_dim(force_bias, lax.axis_index("orb") * per_group, per_group, 1)
    partial_energy = jnp.sum(own_bias * own_bias, axis=1) - pairs_sum
    total_energy = lax.psum(partial_energy, ("chol", "orb"))
    vectors_all = chol_local * lax.axis_size("chol")
    energy = one_body + 0.5 / vectors_all * total_energy
    return (walkers_out, energy)


def solution(mesh):
    return jax.shard_map(
        body,
        mesh=mesh,
        in_specs=(
            P("chol", None, "orb"),
            P(None, None, "orb"),
            P("chol", "orb", None),
            P("chol", None, "orb"),
            P(None, "orb"),
            P(None, "chol"),
        ),
        out_specs=(P("chol", None, "orb"), P()),
        check_vma=False,
    )
```

profile of v0, /device:TPU:1, one launch (start us, length us, event | category | flops | bytes accessed | tf_op | source)
XLA Modules:
  0.0 519.2 jit_solution(7650065071792676428)
XLA Ops:
  7.2 0.0 copy-start
  7.2 0.0 all-gather.5.cloned.1.call-start
  7.2 2.1 copy.17
  9.4 0.0 all-gather.5.cloned.1.call-update
  9.4 11.6 %all-to-all-start = ((bf16[64,200,64]{1,2,0:T(8,128)(2,1)}), bf16[64,200,64]{1,2,0:T(8,128)(2,1)S(1)}, u32[]{:S(2)}, u32[]{:S(2)}) async-start(bf16[64,200,64]{1,2,0:T(8,128)(2,1)} %param.11), calls=%async_computation | async-start | bytes 4194304 | tf_op jit(solution)/shard_map/all_to_all | solution.py:42
  21.0 0.0 copy-start.3
  21.0 0.0 copy-start.2
  21.0 12.0 %copy.29 = bf16[8,8,64,1024]{3,1,2,0:T(8,128)(2,1)} copy(bf16[8,8,64,1024]{3,2,1,0:T(8,128)(2,1)} %bitcast.68) | data formatting | bytes 16777216
  33.0 0.0 copy-done
  33.1 0.0 copy-start.5
  33.1 0.0 copy-done.3
  33.1 0.4 convolution_bitcast_fusion
  33.5 0.0 copy-done.2
  33.5 2.8 fusion.14
  36.3 74.4 %all-reduce = (f32[16,64]{1,0:T(8,128)S(1)}, f32[16]{0:T(128)S(1)}) all-reduce(f32[16,64]{1,0:T(8,128)S(1)} %fusion.14, f32[16]{0:T(128)S(1)} %convolution_bitcast_fusion), channel_id=1, replica_groups=mesh['chol'=16,'orb'=16] {'orb'}, use_global_device_ids=true, to_apply=%region_0.0 | all-reduce | flops 1040 | bytes 8320 | tf_op jit(solution)/shard_map/psum | solution.py:21
  110.8 0.0 copy-done.5
  110.8 6.5 %fusion.19 = f32[16,65536]{1,0:T(8,128)} fusion(bf16[64,65536]{1,0:T(8,128)(2,1)} %bitcast.66, f32[16,64]{1,0:T(8,128)S(1)} %copy-done.5, f32[16,64]{1,0:T(8,128)S(1)} %get-tuple-element.41), kind=kOutput, calls=%fused_computation.29 | convolution fusion | flops 134219776 | bytes 12591104 | tf_op jit(solution)/shard_map/dot_general | solution.py:24
  117.3 0.0 copy-start.4
  117.3 91.4 %all-reduce.2 = bf16[16,65536]{1,0:T(8,128)(2,1)} all-reduce(f32[16,65536]{1,0:T(8,128)} %fusion.19), channel_id=1, replica_groups=mesh['chol'=16,'orb'=16] {'chol'}, use_global_device_ids=true, to_apply=%region_1.0 | all-reduce | flops 1048576 | bytes 6291456 | tf_op jit(solution)/shard_map/psum | solution.py:25
  208.7 2.0 convert_reduce_fusion
  210.7 0.1 convert_element_type.70
  210.8 0.2 multiply_reduce_fusion
  211.0 0.0 copy-done.4
  211.0 36.7 %all_gather.15 = bf16[1,200,1024]{1,2,0:T(8,128)(2,1)S(1)} all-gather(bf16[1,200,64]{1,2,0:T(8,128)(2,1)S(1)} %copy-done.4), channel_id=1, replica_groups=mesh['chol'=16,'orb'=16] {'orb'}, dimensions={2}, use_global_device_ids=true | all-gather | bytes 435200 | tf_op jit(solution)/shard_map/all_gather | solution.py:35
  247.7 0.2 convolution_convert_fusion
  247.9 31.4 %all-gather = bf16[200,1024]{0,1:T(8,128)(2,1)S(1)} all-gather(bf16[200,64]{0,1:T(8,128)(2,1)S(1)} %bitcast.70), channel_id=2, replica_groups=mesh['chol'=16,'orb'=16] {'orb'}, dimensions={1}, use_global_device_ids=true | all-gather | bytes 435200 | tf_op jit(solution)/shard_map/all_gather | solution.py:35
  279.3 0.2 fusion.7
  279.5 33.3 %all-gather.1 = bf16[200,1024]{0,1:T(8,128)(2,1)S(1)} all-gather(bf16[200,64]{0,1:T(8,128)(2,1)S(1)} %fusion.7), channel_id=3, replica_groups=mesh['chol'=16,'orb'=16] {'orb'}, dimensions={1}, use_global_device_ids=true | all-gather | bytes 435200 | tf_op jit(solution)/shard_map/all_gather | solution.py:35
  312.9 0.2 fusion.8
  313.1 34.3 %all-gather.2 = bf16[200,1024]{0,1:T(8,128)(2,1)} all-gather(bf16[200,64]{0,1:T(8,128)(2,1)S(1)} %fusion.8), channel_id=4, replica_groups=mesh['chol'=16,'orb'=16] {'orb'}, dimensions={1}, use_global_device_ids=true | all-gather | bytes 435200 | tf_op jit(solution)/shard_map/all_gather | solution.py:35
  347.3 0.0 all-to-all-done
  347.3 0.0 copy-start.1
  347.3 1.4 copy-done.1
  348.7 1.7 copy.19
  350.5 2.3 copy.21
  352.8 0.0 all-gather.5.cloned.1.call-done
  352.8 11.9 %copy.22 = bf16[16,200,1024]{2,1,0:T(8,128)(2,1)} copy(bf16[16,200,1024]{1,0,2:T(8,128)(2,1)} %all-gather.5.cloned.1.call-done) | data formatting | bytes 13107200 | tf_op jit(solution)/shard_map/while | solution.py:51
  364.7 42.1 %while.10 = (s32[]{:T(128)}, f32[4,16]{1,0:T(4,128)S(1)}, bf16[4,200,1024]{2,1,0:T(8,128)(2,1)}, bf16[16,200,1024]{2,1,0:T(8,128)(2,1)}, s32[]{:T(128)}, /*index=5*/s32[]{:T(128)}) while((s32[]{:T(128)}, f32[4,16]{1,0:T(4,128)S(1)}, bf16[4,200,1024]{2,1,0:T(8,128)(2,1)}, bf16[16,200,1024]{2,1,0:T(8,128)(2,1)}, s32[]{:T(128)}, ...), condition=%wide.region_5.6_spmd, body=%wide.region_4.5_spmd.sunk | while | flops 1312000000 | bytes 19763976 | solution.py:51
  364.7 4.9 fusion.37
  369.6 3.3 copy.41
  372.9 2.3 fusion.38
  375.2 4.9 fusion.37
  380.1 3.3 copy.41
  383.4 2.3 fusion.38
  385.8 4.9 fusion.37
  390.7 3.3 copy.41
  393.9 2.3 fusion.38
  396.3 4.9 fusion.37
  401.2 3.3 copy.41
  404.5 2.3 fusion.38
  406.9 1.9 fusion.13
  408.7 103.1 %psum.31 = f32[16]{0:T(128)S(1)} all-reduce(f32[16]{0:T(128)S(1)} %sub.7), channel_id=1, replica_groups=mesh['chol'=16,'orb'=16] {'chol','orb'}, use_global_device_ids=true, to_apply=%region_7.8 | all-reduce | flops 16 | bytes 128 | tf_op jit(solution)/shard_map/psum | solution.py:54
  511.8 0.5 multiply_add_fusion
  (7 shorter events, 0.2 us)
Async XLA Ops:
  7.2 25.9 %copy-start = (bf16[200,64]{0,1:T(8,128)(2,1)S(1)}, bf16[200,64]{0,1:T(8,128)(2,1)}, u32[]{:S(2)}) copy-start(bf16[200,64]{0,1:T(8,128)(2,1)} %param.12) | copy-start | bytes 76804
  7.2 345.6 %all-gather.5.cloned.1.call-start = ((), (), s32[]{:S(2)}) async-start(), calls=%async_computation.1 | async-start | bytes 8912896 | tf_op jit(solution)/shard_map/all_gather | solution.py:43
  9.4 338.0 %all-to-all-start = ((bf16[64,200,64]{1,2,0:T(8,128)(2,1)}), bf16[64,200,64]{1,2,0:T(8,128)(2,1)S(1)}, u32[]{:S(2)}, u32[]{:S(2)}) async-start(bf16[64,200,64]{1,2,0:T(8,128)(2,1)} %param.11), calls=%async_computation | async-start | bytes 4194304 | tf_op jit(solution)/shard_map/all_to_all | solution.py:42
  21.0 12.1 %copy-start.3 = (bf16[16,200,64]{1,2,0:T(8,128)(2,1)S(1)}, bf16[16,200,64]{1,2,0:T(8,128)(2,1)}, u32[]{:S(2)}) copy-start(bf16[16,200,64]{1,2,0:T(8,128)(2,1)} %param.9) | copy-start | bytes 1228804
  21.0 12.5 %copy-start.2 = (bf16[64,200,64]{1,2,0:T(8,128)(2,1)S(1)}, bf16[64,200,64]{1,2,0:T(8,128)(2,1)}, u32[]{:S(2)}) copy-start(bf16[64,200,64]{1,2,0:T(8,128)(2,1)} %param.11) | copy-start | bytes 4915204
  33.1 77.7 %copy-start.5 = (f32[16,64]{1,0:T(8,128)S(1)}, f32[16,64]{1,0:T(8,128)}, u32[]{:S(2)}) copy-start(f32[16,64]{1,0:T(8,128)} %param.13) | copy-start | bytes 12292
  117.3 93.7 %copy-start.4 = (bf16[1,200,64]{1,2,0:T(8,128)(2,1)S(1)}, bf16[1,200,64]{1,2,0:T(8,128)(2,1)}, u32[]{:S(2)}) copy-start(bf16[1,200,64]{1,2,0:T(8,128)(2,1)} %param.8) | copy-start | bytes 76804
  347.3 1.4 copy-start.1
Sparse Core Ops, SparseCore 0:
  10.6 182.7 all-gather.4
where the time goes:
time: 520 us; the launch traced here: 519 us
  blocking collectives  405 us (78%)
  local copies, waits for them, and re-layouts  46.8 us (9%)
  matrix products  31.9 us (6%)
  between operations  14.1 us (3%)
  starting transfers between devices  11.6 us (2%)
  other arithmetic  10.1 us (2%)
    all_gather x4, blocking collectives, body(): lax.all_gather(current, 'orb', axis=2, tiled=True)  136 us
    psum x1, blocking collectives, body(): total_energy = lax.psum(partial_energy, ('chol', 'orb'))  103 us
    psum x1, blocking collectives, body(): summed_operator = lax.psum(partial_operator, 'chol')  91.4 us
    psum x1, blocking collectives, body(): force_bias, one_body = lax.psum((bias_part, one_part), 'orb')  74.4 us
    dot_general x4, matrix products, vector_pairs(): jnp.einsum('en,wfn->wef', single, theta_full, preferred_element_type=jnp....  19.6 us
    unnamed x14, local copies, waits for them, and re-layouts  15.6 us
    while x2, local copies, waits for them, and re-layouts, body(): pairs_sum = jnp.sum(lax.map(vector_pairs, rotated_mine), axis=0)  14.2 us
    while x4, local copies, waits for them, and re-layouts  13 us
  transfers between devices with their start and end apart: 2, of which 0 were waited for; matrix products, arithmetic and copies ran while one was open for 6% of the time, Pallas kernels for 0%

commit v1 on v0

v1 whole, which is shorter than its diff:
```python
import jax
import jax.numpy as jnp
from jax import lax
from jax.experimental import pallas as pl
from jax.experimental.pallas import tpu as pltpu
from jax.sharding import PartitionSpec as P

ORDER = 4
MESH = pl.DeviceIdType.MESH
F32 = jnp.float32
BF16 = jnp.bfloat16
VECTORS = 1024
TILE = 16


def iota(shape, dim):
    return lax.broadcasted_iota(jnp.int32, shape, dim)


def kernel(phi, th, cv, cr, hc, aux, wout, en,
           crv, cvv, thv, tbuf, abuf, a_t, fbx, smat, opart, osib, osum, opl, obuf, ored,
           pbuf, term, acc, res, land, x_buf, ebuf, e2buf,
           s_loc, s_t1, r_t1, s_tx, r_tx, s_ty, r_ty, s_tf, r_tf, s_phi, r_phi,
           s_a, r_a, s_as, r_as, s_fb, r_fb, s_os, r_os, s_op, r_op, s_od, r_od,
           s_w, r_w, s_e1, r_e1, s_e2, r_e2):
    c = lax.axis_index("chol")
    o = lax.axis_index("orb")
    core = lax.rem(c, 2)
    xl = c // 8
    y = lax.rem(c // 2, 4)
    j = c // 2
    sib = (2 * j + 1 - core, o)
    yp = lax.rem(y + 1, 4)
    ym = lax.rem(y + 3, 4)
    y2 = lax.rem(y + 2, 4)

    def plane(jj):
        return (2 * jj + core, o)

    xpart = plane((1 - xl) * 4 + y)
    dest = core * 8 + lax.rem(2 * y + xl + 4 * core, 8)

    def rcopy(src, dst, ss, rs, dev):
        return pltpu.make_async_remote_copy(
            src_ref=src, dst_ref=dst, send_sem=ss, recv_sem=rs, device_id=dev, device_id_type=MESH)

    def orb_peer(i):
        return lax.rem(o + i, 16)

    def plane_peer(i):
        return lax.rem(j + i, 8)

    cp_cr = pltpu.make_async_copy(cr, crv, s_loc.at[0])
    cp_cr.start()
    cp_th = pltpu.make_async_copy(th, thv, s_loc.at[1])
    cp_th.start()
    cp_cv = pltpu.make_async_copy(cv, cvv, s_loc.at[2])
    cp_cv.start()

    bar = pltpu.get_barrier_semaphore()

    def sig_orb(i, _):
        pl.semaphore_signal(bar, inc=1, device_id=(c, orb_peer(i)), device_id_type=MESH)
        return 0

    def sig_chol(i, _):
        pl.semaphore_signal(bar, inc=1, device_id=(lax.rem(c + i, 16), o), device_id_type=MESH)
        return 0

    lax.fori_loop(1, 16, sig_orb, 0)
    lax.fori_loop(1, 16, sig_chol, 0)
    pl.semaphore_wait(bar, 30)

    cp_own_t = pltpu.make_async_copy(th.at[c], tbuf.at[j, o], s_loc.at[3])
    cp_own_t.start()

    def t1(i):
        return rcopy(th.at[c], tbuf.at[j, o], s_t1.at[i], r_t1.at[o], (c, orb_peer(i)))

    def t1_start(i, _):
        t1(i).start()
        return 0

    lax.fori_loop(1, 16, t1_start, 0)

    cp_phi = rcopy(phi, pbuf.at[o], s_phi, r_phi.at[o], (c, dest))
    cp_phi_own = pltpu.make_async_copy(phi, pbuf.at[o], s_loc.at[4])

    @pl.when(o != dest)
    def _():
        cp_phi.start()

    @pl.when(o == dest)
    def _():
        cp_phi_own.start()

    def a2a(i):
        p = orb_peer(i)
        return rcopy(cr.at[pl.ds(4 * p, 4)], abuf.at[core, o], s_a.at[i], r_a.at[o], (c, p))

    def a2a_start(i, _):
        a2a(i).start()
        return 0

    cp_own_a = pltpu.make_async_copy(cr.at[pl.ds(4 * o, 4)], abuf.at[core, o], s_loc.at[5])
    cp_own_a.start()

    cp_th.wait()
    cp_cr.wait()
    mask = (iota((64, 256), 0) == lax.rem(iota((64, 256), 1), 64)).astype(F32)

    def split_dot(z, ind):
        hi = z.astype(BF16)
        lo = (z - hi.astype(F32)).astype(BF16)
        return (jnp.dot(hi, ind, preferred_element_type=F32)
                + jnp.dot(lo, ind, preferred_element_type=F32))

    def fb_step(i, tot):
        rhs = crv[pl.ds(4 * i, 4)].reshape(256, 200)
        z = lax.dot_general(thv[...].reshape(1024, 200), rhs, (((1,), (1,)), ((), ())),
                            preferred_element_type=F32)
        z = jnp.sum(z.reshape(16, 64, 256) * mask[None], axis=1)
        ind = (iota((256, 128), 1) == 4 * i + iota((256, 128), 0) // 64).astype(BF16)
        return tot + split_dot(z, ind)

    fb_part = lax.fori_loop(0, 16, fb_step, jnp.zeros((16, 128), F32))
    z1 = lax.dot_general(thv[...].reshape(1024, 200), hc[...], (((1,), (1,)), ((), ())),
                         preferred_element_type=F32)
    z1 = jnp.sum(z1.reshape(16, 64, 64) * mask[None, :, :64], axis=1)
    one_part = jnp.sum(z1, axis=1, keepdims=True)
    fbx[o] = fb_part + jnp.where(iota((16, 128), 1) == 64, one_part, 0.0)

    def fb_copy(i):
        return rcopy(fbx.at[o], fbx.at[o], s_fb.at[i], r_fb.at[o], (c, orb_peer(i)))

    def fb_start(i, _):
        fb_copy(i).start()
        return 0

    lax.fori_loop(1, 16, fb_start, 0)
    lax.fori_loop(1, 16, a2a_start, 0)

    def fb_wait(i, _):
        p = orb_peer(i)
        rcopy(fbx.at[p], fbx.at[p], s_fb.at[i], r_fb.at[p], (c, p)).wait_recv()
        return 0

    lax.fori_loop(1, 16, fb_wait, 0)
    fb_all = jnp.sum(fbx[...], axis=0)
    shifted = (aux[...] - fb_all[:, :64]).astype(BF16)

    row = iota((256, 16), 0)
    ew = (iota((256, 16), 1) == 2 * lax.rem(row // TILE, 8) + row // 128).astype(BF16)
    ea = (iota((64, 1024), 0) == iota((64, 1024), 1) // TILE).astype(BF16)
    spread = jnp.dot(jnp.dot(ew, shifted, preferred_element_type=F32).astype(BF16), ea,
                     preferred_element_type=F32)
    diag = lax.rem(iota((256, 1024), 0), TILE) == lax.rem(iota((256, 1024), 1), TILE)
    smat[...] = jnp.where(diag, spread, 0.0).astype(BF16)
    cp_cv.wait()

    def os_copy(t):
        return rcopy(opart.at[t, 1 - core], osib.at[t], s_os.at[t], r_os.at[t], sib)

    def op_step(t, _):
        def op_half(h, _):
            cols = pl.ds(pl.multiple_of(h * 256, 256), 256)
            rt = cvv[:, pl.ds(pl.multiple_of(TILE * t, TILE), TILE), cols].reshape(1024, 256)
            opart[t, :, :, :, cols] = jnp.dot(
                smat[...], rt, preferred_element_type=F32).astype(BF16).reshape(2, 8, TILE, 256)
            return 0
        lax.fori_loop(0, 4, op_half, 0)
        os_copy(t).start()
        return 0

    lax.fori_loop(0, 4, op_step, 0)

    cp_own_t.wait()

    def t1_wait(i, _):
        p = orb_peer(i)
        rcopy(th.at[c], tbuf.at[j, p], s_t1.at[i], r_t1.at[p], (c, p)).wait_recv()
        return 0

    lax.fori_loop(1, 16, t1_wait, 0)
    jx = (1 - xl) * 4 + y
    cp_tx = rcopy(tbuf.at[j], tbuf.at[j], s_tx, r_tx, xpart)
    cp_tx.start()

    def ty(slot, which, up):
        to = yp if up else ym
        return rcopy(tbuf.at[slot], tbuf.at[slot], s_ty.at[which, int(up)], r_ty.at[which, int(up)],
                     plane(xl * 4 + to))

    ty(j, 0, True).start()
    ty(j, 0, False).start()

    def op_copy(t, i):
        jj = plane_peer(i)
        return rcopy(osum.at[t, jj], opl.at[t, j], s_op.at[t, i], r_op.at[t, j], plane(jj))

    def sum_step(t, _):
        os_copy(t).wait_recv()
        osum[t] = (opart[t, core].astype(F32) + osib[t].astype(F32)).astype(BF16)
        opl[t, j] = osum[t, j]

        def go(i, _):
            op_copy(t, i).start()
            return 0
        lax.fori_loop(1, 8, go, 0)
        return 0

    lax.fori_loop(0, 4, sum_step, 0)

    rcopy(tbuf.at[jx], tbuf.at[jx], s_tx, r_tx, xpart).wait_recv()
    ty(jx, 1, True).start()
    ty(jx, 1, False).start()

    od_copy = lambda t: rcopy(ored.at[t], obuf.at[o, t], s_od.at[t], r_od.at[o, t], (c, dest))

    def red_step(t, _):
        def w(i, _):
            jj = plane_peer(i)
            rcopy(osum.at[t, jj], opl.at[t, jj], s_op.at[t, i], r_op.at[t, jj], plane(jj)).wait_recv()
            return 0
        lax.fori_loop(1, 8, w, 0)
        tot = opl[t, 0].astype(F32)
        for q in range(1, 8):
            tot = tot + opl[t, q].astype(F32)

        @pl.when(o != dest)
        def _():
            ored[t] = tot.astype(BF16)
            od_copy(t).start()

        @pl.when(o == dest)
        def _():
            obuf[o, t] = tot.astype(BF16)
        return 0

    lax.fori_loop(0, 4, red_step, 0)

    def tf(which, up):
        source = ym if up else yp
        slot = (xl if which == 0 else 1 - xl) * 4 + source
        h = 0 if up else 8
        to = yp if up else ym
        piece = tbuf.at[slot, pl.ds(h, 8)]
        return rcopy(piece, piece, s_tf.at[which, int(up)], r_tf.at[which, int(up)], plane(xl * 4 + to))

    for which in (0, 1):
        for up in (True, False):
            slot = (xl if which == 0 else 1 - xl) * 4 + (ym if up else yp)
            rcopy(tbuf.at[slot], tbuf.at[slot], s_ty.at[which, int(up)], r_ty.at[which, int(up)], sib).wait_recv()
            tf(which, up).start()

    def as_copy(p):
        return rcopy(abuf.at[core, p], abuf.at[core, p], s_as.at[p], r_as.at[p], sib)

    cp_own_a.wait()
    as_copy(o).start()

    def a_fwd(i, _):
        p = lax.rem(o - i + 16, 16)
        rcopy(cr.at[pl.ds(4 * p, 4)], abuf.at[core, p], s_a.at[i], r_a.at[p], (c, p)).wait_recv()
        as_copy(p).start()
        return 0

    lax.fori_loop(1, 16, a_fwd, 0)

    @pl.when(o == dest)
    def _():
        cp_phi_own.wait()

        def w(i, _):
            p = orb_peer(i)
            rcopy(phi, pbuf.at[p], s_phi, r_phi.at[p], (c, dest)).wait_recv()

            def wt(t, _):
                rcopy(ored.at[t], obuf.at[p, t], s_od.at[t], r_od.at[p, t], (c, dest)).wait_recv()
                return 0
            lax.fori_loop(0, 4, wt, 0)
            return 0
        lax.fori_loop(1, 16, w, 0)
        term[0] = pbuf[...].reshape(1024, 200)
        acc[...] = pbuf[...].reshape(1024, 200).astype(F32)
        for degree in range(1, ORDER + 1):
            src, dst = (degree - 1) % 2, degree % 2

            def mm(b, _):
                rows = pl.ds(pl.multiple_of(b * 256, 256), 256)
                lhs = obuf[pl.ds(4 * b, 4)].reshape(256, 1024)
                prod = jnp.dot(lhs, term[src], preferred_element_type=F32)
                new = (prod / degree).astype(BF16)
                term[dst, rows] = new
                acc[rows] = acc[rows] + new.astype(F32)
                return 0
            lax.fori_loop(0, 4, mm, 0)
        res[...] = acc[...].astype(BF16).reshape(16, 64, 200)

        def send(i, _):
            p = orb_peer(i)
            rcopy(res.at[p], land, s_w.at[i], r_w, (c, p)).start()
            return 0
        lax.fori_loop(1, 16, send, 0)

    for up in (True, False):
        for which in (0, 1):
            slot = (xl if which == 0 else 1 - xl) * 4 + y2
            piece = tbuf.at[slot, pl.ds(0 if up else 8, 8)]
            rcopy(piece, piece, s_tf.at[which, int(up)], r_tf.at[which, int(up)], sib).wait_recv()

    def as_wait(p, _):
        rcopy(abuf.at[1 - core, p], abuf.at[1 - core, p], s_as.at[p], r_as.at[p], sib).wait_recv()
        return 0

    lax.fori_loop(0, 16, as_wait, 0)

    def tr_step(i, _):
        for h in range(8):
            blk = abuf[i // 4, pl.ds(2 * h, 2), lax.rem(i, 4)].reshape(128, 200)
            a_t[i, :, 128 * h:128 * h + 128] = blk.T
        return 0

    lax.fori_loop(0, 8, tr_step, 0)
    eye = iota((200, 200), 0) == iota((200, 200), 1)

    def w_step(jj, tot):
        b = tbuf[jj].reshape(1024, 200)

        def half(h, _):
            x_buf[pl.ds(4 * h, 4)] = jnp.dot(
                a_t[pl.ds(4 * h, 4)].reshape(800, 1024), b,
                preferred_element_type=F32).astype(BF16).reshape(4, 200, 200)
            return 0
        lax.fori_loop(0, 2, half, 0)

        def sq(i, d):
            xb = x_buf[i]
            return d + jnp.dot(xb, xb, preferred_element_type=F32)
        d = lax.fori_loop(0, 8, sq, jnp.zeros((200, 200), F32))
        value = jnp.sum(jnp.where(eye, d, 0.0))
        return tot + jnp.where(iota((8, 128), 1) == 2 * jj + core, value, 0.0)

    pairs = lax.fori_loop(0, 8, w_step, jnp.zeros((8, 128), F32))

    ebuf[o] = pairs

    def e1(i):
        return rcopy(ebuf.at[o], ebuf.at[o], s_e1.at[i], r_e1.at[o], (c, orb_peer(i)))

    def e1_start(i, _):
        e1(i).start()
        return 0

    lax.fori_loop(1, 16, e1_start, 0)

    def e1_wait(i, _):
        p = orb_peer(i)
        rcopy(ebuf.at[p], ebuf.at[p], s_e1.at[i], r_e1.at[p], (c, p)).wait_recv()
        return 0

    @pl.when(o == dest)
    def _():
        wout[...] = res[o]

    @pl.when(o != dest)
    def _():
        rcopy(land, land, s_w.at[0], r_w, (c, dest)).wait_recv()
        wout[...] = land[...]

    lax.fori_loop(1, 16, e1_wait, 0)
    bias = jnp.where(iota((16, 128), 1) < 64, fb_all, 0.0)
    coulomb = jnp.sum(bias * bias, axis=1, keepdims=True)
    wl = iota((16, 128), 0) == iota((16, 128), 1)
    e_row = jnp.sum(jnp.where(wl, coulomb, 0.0), axis=0, keepdims=True)
    one_row = jnp.sum(jnp.where(wl, fb_all[:, 64:65], 0.0), axis=0, keepdims=True)
    e2buf[c] = e_row - jnp.sum(ebuf[...], axis=0)

    def e2(i):
        return rcopy(e2buf.at[c], e2buf.at[c], s_e2.at[i], r_e2.at[c], (lax.rem(c + i, 16), o))

    def e2_start(i, _):
        e2(i).start()
        return 0

    lax.fori_loop(1, 16, e2_start, 0)

    def e2_wait(i, _):
        p = lax.rem(c + i, 16)
        rcopy(e2buf.at[p], e2buf.at[p], s_e2.at[i], r_e2.at[p], (p, o)).wait_recv()
        return 0

    lax.fori_loop(1, 16, e2_wait, 0)
    en[...] = one_row + 0.5 / VECTORS * jnp.sum(e2buf[...], axis=0)

    def sent(i, _):
        t1(i).wait_send()
        a2a(i).wait_send()
        fb_copy(i).wait_send()
        e1(i).wait_send()
        e2(i).wait_send()
        return 0

    lax.fori_loop(1, 16, sent, 0)

    def sent_as(p, _):
        as_copy(p).wait_send()
        return 0

    lax.fori_loop(0, 16, sent_as, 0)
    cp_tx.wait_send()
    for which in (0, 1):
        for up in (True, False):
            ty(j if which == 0 else jx, which, up).wait_send()
            tf(which, up).wait_send()

    def sent_o(t, _):
        os_copy(t).wait_send()

        def go(i, _):
            op_copy(t, i).wait_send()
            return 0
        lax.fori_loop(1, 8, go, 0)
        return 0

    lax.fori_loop(0, 4, sent_o, 0)

    @pl.when(o != dest)
    def _():
        cp_phi.wait_send()

        def go(t, _):
            od_copy(t).wait_send()
            return 0
        lax.fori_loop(0, 4, go, 0)

    @pl.when(o == dest)
    def _():
        def go(i, _):
            p = orb_peer(i)
            rcopy(res.at[p], land, s_w.at[i], r_w, (c, p)).wait_send()
            return 0
        lax.fori_loop(1, 16, go, 0)


def body(phi_walkers, theta_half, chol_vectors, chol_rotated, hcore_rotated, aux_fields):
    flip = lambda v: jnp.swapaxes(v, -1, -2)
    vm = pl.BlockSpec(memory_space=pltpu.VMEM)
    hbm = pl.BlockSpec(memory_space=pl.ANY)
    dma = pltpu.SemaphoreType.DMA
    sems = [(6,), (16,), (16,), (), (), (2, 2), (2, 2), (2, 2), (2, 2), (), (16,),
            (16,), (16,), (16,), (16,), (16,), (16,), (4,), (4,), (4, 8), (4, 8), (4,), (16, 4),
            (16,), (), (16,), (16,), (16,), (16,)]
    wout, en = pl.pallas_call(
        kernel,
        out_shape=(jax.ShapeDtypeStruct((64, 200), BF16), jax.ShapeDtypeStruct((8, 128), F32)),
        in_specs=[hbm, hbm, hbm, hbm, vm, vm],
        out_specs=(vm, vm),
        scratch_shapes=[
            pltpu.VMEM((64, 64, 200), BF16),
            pltpu.VMEM((64, 64, 1024), BF16),
            pltpu.VMEM((16, 64, 200), BF16),
            pltpu.VMEM((8, 16, 64, 200), BF16),
            pltpu.VMEM((2, 16, 4, 64, 200), BF16),
            pltpu.VMEM((8, 200, 1024), BF16),
            pltpu.VMEM((16, 16, 128), F32),
            pltpu.VMEM((256, 1024), BF16),
            pltpu.VMEM((4, 2, 8, TILE, 1024), BF16),
            pltpu.VMEM((4, 8, TILE, 1024), BF16),
            pltpu.VMEM((4, 8, TILE, 1024), BF16),
            pltpu.VMEM((4, 8, TILE, 1024), BF16),
            pltpu.VMEM((16, 4, TILE, 1024), BF16),
            pltpu.VMEM((4, TILE, 1024), BF16),
            pltpu.VMEM((16, 64, 200), BF16),
            pltpu.VMEM((2, 1024, 200), BF16),
            pltpu.VMEM((1024, 200), F32),
            pltpu.VMEM((16, 64, 200), BF16),
            pltpu.VMEM((64, 200), BF16),
            pltpu.VMEM((8, 200, 200), BF16),
            pltpu.VMEM((16, 8, 128), F32),
            pltpu.VMEM((16, 8, 128), F32),
        ] + [dma(s) if s else dma for s in sems],
        compiler_params=pltpu.CompilerParams(
            collective_id=0, has_side_effects=True, vmem_limit_bytes=56 << 20),
        cost_estimate=pl.CostEstimate(flops=14 * 10**9, bytes_accessed=12 * 10**6, transcendentals=0),
    )(
        flip(phi_walkers)[0],
        flip(theta_half),
        chol_vectors,
        flip(chol_rotated),
        flip(hcore_rotated),
        aux_fields,
    )
    return flip(wout)[None], en[0, :16]


def solution(mesh):
    return jax.shard_map(
        body,
        mesh=mesh,
        in_specs=(
            P("chol", None, "orb"),
            P(None, None, "orb"),
            P("chol", "orb", None),
            P("chol", None, "orb"),
            P(None, "orb"),
            P(None, "chol"),
        ),
        out_specs=(P("chol", None, "orb"), P()),
        check_vma=False,
    )
```

time: 520 us -> 145 us (0.28)
  blocking collectives: 405 us -> 0 us
  Pallas kernels: 0 us -> 142 us
  local copies, waits for them, and re-layouts: 46.8 us -> 2.57 us
  matrix products: 31.9 us -> 0 us
  between operations: 14.1 us -> 0.64 us
  starting transfers between devices: 11.6 us -> 0 us
  other arithmetic: 10.1 us -> 0 us
    psum x3 -> x0, blocking collectives: 269 us -> none  [the longest x1 103 us: body(): total_energy = lax.psum(partial_energy, ('chol', 'orb'))]
    pallas_call x0 -> x1, Pallas kernels: none -> 142 us  [body(): pl.pallas_call(kernel, out_shape=(jax.ShapeDtypeStruct((64, 200), BF16),...]
    all_gather x4 -> x0, blocking collectives: 136 us -> none  [body(): lax.all_gather(current, 'orb', axis=2, tiled=True)]
    dot_general x11 -> x0, matrix products: 31.9 us -> none  [the longest x4 19.6 us: vector_pairs(): jnp.einsum('en,wfn->wef', single, theta_full, preferred_element_type=jnp....]
    while x6 -> x0, local copies, waits for them, and re-layouts: 27.3 us -> none  [the longest x2 14.2 us: body(): pairs_sum = jnp.sum(lax.map(vector_pairs, rotated_mine), axis=0)]
    unnamed x14 -> x1, local copies, waits for them, and re-layouts: 15.6 us -> 1.37 us
    all_to_all x1 -> x0, starting transfers between devices: 11.6 us -> none  [body(): lax.all_to_all(chol_rotated, 'orb', split_axis=0, concat_axis=2, tiled=True)]
    dot_general x4 -> x0, other arithmetic: 9.34 us -> none  [vector_pairs(): return jnp.einsum('wef,wfe->w', pair_matrix, pair_matrix)]
  transfers between devices with their start and end apart: 2 -> 0, of which waited for: 0 -> 0; matrix products, arithmetic and copies ran while one was open for 6% -> 0% of each run, Pallas kernels for 0% -> 0%
where the time goes in v1:
time: 145 us
  Pallas kernels  142 us (98%)
  local copies, waits for them, and re-layouts  2.57 us (2%)
    pallas_call x1, Pallas kernels, body(): pl.pallas_call(kernel, out_shape=(jax.ShapeDtypeStruct((64, 200), BF16),...  142 us

profile of v1, /device:TPU:1, one launch (start us, length us, event | category | flops | bytes accessed | tf_op | source)
XLA Modules:
  0.0 144.8 jit_solution(4958145990747065203)
XLA Ops:
  0.6 141.6 %shard_map.77 = (bf16[64,200]{1,0:T(8,128)(2,1)}, f32[8,128]{1,0:T(8,128)}) custom-call(bf16[64,200]{1,0:T(8,128)(2,1)} %bitcast.14, bf16[16,64,200]{2,1,0:T(8,128)(2,1)} %bitcast.13, bf16[64,64,1024]{2,1,0:T(8,128)(2,1)} %cv.1, bf16[64,64,200]{2,1,0:T(8,128)(2,1)} %bitcast.12, bf16[64,200]{1,0:T(8,128)(2,1)} %bitcast.15, f32[16,64]{1,0:T(8,128)} %aux.1), custom_call_target="tpu_custom_call" | custom-call | flops 14000000000 | bytes 12000000 | tf_op jit(solution)/shard_map/pallas_call | solution.py:454
  142.2 1.2 slice_bitcast_fusion
  143.4 1.4 copy.9

commit v2 on v1

--- a/solution.py
+++ b/solution.py
@@ -18,9 +18,9 @@
 
 
 def kernel(phi, th, cv, cr, hc, aux, wout, en,
-           crv, cvv, thv, tbuf, abuf, a_t, fbx, smat, opart, osib, osum, opl, obuf, ored,
-           pbuf, term, acc, res, land, x_buf, ebuf, e2buf,
-           s_loc, s_t1, r_t1, s_tx, r_tx, s_ty, r_ty, s_tf, r_tf, s_phi, r_phi,
+           crv, cvv, thv, zsum, tbuf, pk, abuf, a_t, fbx, smat, opart, osib, osum, opl, obuf, ored,
+           pbuf, term, acc, res, land, x_up, x_lo, ebuf, e2buf,
+           s_loc, s_cv, s_t1, r_t1, s_tx, r_tx, s_ty, r_ty, s_tf, r_tf, s_phi, r_phi,
            s_a, r_a, s_as, r_as, s_fb, r_fb, s_os, r_os, s_op, r_op, s_od, r_od,
            s_w, r_w, s_e1, r_e1, s_e2, r_e2):
     c = lax.axis_index("chol")
@@ -54,8 +54,9 @@
     cp_cr.start()
     cp_th = pltpu.make_async_copy(th, thv, s_loc.at[1])
     cp_th.start()
-    cp_cv = pltpu.make_async_copy(cv, cvv, s_loc.at[2])
-    cp_cv.start()
+
+    def cv_copy(q):
+        return pltpu.make_async_copy(cv.at[pl.ds(8 * q, 8)], cvv.at[pl.ds(8 * q, 8)], s_cv.at[q])
 
     bar = pltpu.get_barrier_semaphore()
 
@@ -74,14 +75,17 @@
     cp_own_t = pltpu.make_async_copy(th.at[c], tbuf.at[j, o], s_loc.at[3])
     cp_own_t.start()
 
+    def z_peer(i):
+        return (o // 8) * 8 + lax.rem(o + i, 8)
+
     def t1(i):
-        return rcopy(th.at[c], tbuf.at[j, o], s_t1.at[i], r_t1.at[o], (c, orb_peer(i)))
+        return rcopy(th.at[c], tbuf.at[j, o], s_t1.at[i], r_t1.at[o], (c, z_peer(i)))
 
     def t1_start(i, _):
         t1(i).start()
         return 0
 
-    lax.fori_loop(1, 16, t1_start, 0)
+    lax.fori_loop(1, 8, t1_start, 0)
 
     cp_phi = rcopy(phi, pbuf.at[o], s_phi, r_phi.at[o], (c, dest))
     cp_phi_own = pltpu.make_async_copy(phi, pbuf.at[o], s_loc.at[4])
@@ -96,39 +100,68 @@
 
     def a2a(i):
         p = orb_peer(i)
-        return rcopy(cr.at[pl.ds(4 * p, 4)], abuf.at[core, o], s_a.at[i], r_a.at[o], (c, p))
+        return rcopy(pk.at[p], abuf.at[core, o], s_a.at[i], r_a.at[o], (c, p))
 
     def a2a_start(i, _):
         a2a(i).start()
         return 0
 
-    cp_own_a = pltpu.make_async_copy(cr.at[pl.ds(4 * o, 4)], abuf.at[core, o], s_loc.at[5])
-    cp_own_a.start()
-
     cp_th.wait()
     cp_cr.wait()
-    mask = (iota((64, 256), 0) == lax.rem(iota((64, 256), 1), 64)).astype(F32)
-
-    def split_dot(z, ind):
-        hi = z.astype(BF16)
-        lo = (z - hi.astype(F32)).astype(BF16)
-        return (jnp.dot(hi, ind, preferred_element_type=F32)
-                + jnp.dot(lo, ind, preferred_element_type=F32))
-
-    def fb_step(i, tot):
-        rhs = crv[pl.ds(4 * i, 4)].reshape(256, 200)
+
+    def cv_start(q, _):
+        cv_copy(q).start()
+        return 0
+
+    lax.fori_loop(0, 8, cv_start, 0)
+    def pack(i, _):
+        for v in range(4):
+            pk[i, :, 200 * v:200 * v + 200] = crv[4 * i + v]
+        pk[i, :, 800:] = jnp.zeros((64, 96), BF16)
+        return 0
+
+    lax.fori_loop(0, 16, pack, 0)
+    cp_own_a = pltpu.make_async_copy(pk.at[o], abuf.at[core, o], s_loc.at[5])
+    cp_own_a.start()
+
+    mask = (iota((64, 512), 0) == lax.rem(iota((64, 512), 1), 64)).astype(F32)
+
+    def fb_step(i, _):
+        rhs = crv[pl.ds(8 * i, 8)].reshape(512, 200)
         z = lax.dot_general(thv[...].reshape(1024, 200), rhs, (((1,), (1,)), ((), ())),
                             preferred_element_type=F32)
-        z = jnp.sum(z.reshape(16, 64, 256) * mask[None], axis=1)
-        ind = (iota((256, 128), 1) == 4 * i + iota((256, 128), 0) // 64).astype(BF16)
-        return tot + split_dot(z, ind)
-
-    fb_part = lax.fori_loop(0, 16, fb_step, jnp.zeros((16, 128), F32))
+        zsum[:, pl.ds(pl.multiple_of(512 * i, 512), 512)] = jnp.sum(
+            z.reshape(16, 64, 512) * mask[None], axis=1)
+        return 0
+
+    lax.fori_loop(0, 4, fb_step, 0)
+    cp_own_t.wait()
+
+    def t1x(p):
+        return rcopy(tbuf.at[j, p], tbuf.at[j, p], s_t1.at[8 + lax.rem(p, 8)], r_t1.at[p], (c, lax.rem(o + 8, 16)))
+
+    t1x(o).start()
+
+    def t1_wait(i, _):
+        p = z_peer(i)
+        rcopy(th.at[c], tbuf.at[j, p], s_t1.at[i], r_t1.at[p], (c, p)).wait_recv()
+        t1x(p).start()
+        return 0
+
+    lax.fori_loop(1, 8, t1_wait, 0)
+
+    lax.fori_loop(4, 8, fb_step, 0)
     z1 = lax.dot_general(thv[...].reshape(1024, 200), hc[...], (((1,), (1,)), ((), ())),
                          preferred_element_type=F32)
     z1 = jnp.sum(z1.reshape(16, 64, 64) * mask[None, :, :64], axis=1)
     one_part = jnp.sum(z1, axis=1, keepdims=True)
-    fbx[o] = fb_part + jnp.where(iota((16, 128), 1) == 64, one_part, 0.0)
+    zs = zsum[...]
+    hi = zs.astype(BF16)
+    lo = (zs - hi.astype(F32)).astype(BF16)
+    ind = (iota((4096, 128), 1) == iota((4096, 128), 0) // 64).astype(BF16)
+    both = jnp.dot(jnp.concatenate([hi, lo], axis=0), ind, preferred_element_type=F32)
+    fbx[o] = (both[:16] + both[16:]
+              + jnp.where(iota((16, 128), 1) == 64, one_part, 0.0))
 
     def fb_copy(i):
         return rcopy(fbx.at[o], fbx.at[o], s_fb.at[i], r_fb.at[o], (c, orb_peer(i)))
@@ -139,6 +172,33 @@
 
     lax.fori_loop(1, 16, fb_start, 0)
     lax.fori_loop(1, 16, a2a_start, 0)
+
+    def t1x_wait(i, _):
+        t1x(lax.rem(z_peer(i) + 8, 16)).wait_recv()
+        return 0
+
+    lax.fori_loop(0, 8, t1x_wait, 0)
+    jx = (1 - xl) * 4 + y
+
+    def tx(slot, g):
+        piece = tbuf.at[slot, pl.ds(4 * g, 4)]
+        return rcopy(piece, piece, s_tx.at[g], r_tx.at[g], xpart)
+
+
+    def ty(slot, which, up, g):
+        to = yp if up else ym
+        piece = tbuf.at[slot, pl.ds(4 * g, 4)]
+        return rcopy(piece, piece, s_ty.at[which, int(up), g], r_ty.at[which, int(up), g],
+                     plane(xl * 4 + to))
+
+    def tx_start(g, _):
+        tx(j, g).start()
+        ty(j, 0, True, g).start()
+        ty(j, 0, False, g).start()
+        return 0
+
+    lax.fori_loop(0, 4, tx_start, 0)
+
 
     def fb_wait(i, _):
         p = orb_peer(i)
@@ -156,10 +216,15 @@
                      preferred_element_type=F32)
     diag = lax.rem(iota((256, 1024), 0), TILE) == lax.rem(iota((256, 1024), 1), TILE)
     smat[...] = jnp.where(diag, spread, 0.0).astype(BF16)
-    cp_cv.wait()
-
-    def os_copy(t):
-        return rcopy(opart.at[t, 1 - core], osib.at[t], s_os.at[t], r_os.at[t], sib)
+
+    def cv_wait(q, _):
+        cv_copy(q).wait()
+        return 0
+
+    lax.fori_loop(0, 8, cv_wait, 0)
+
+    def os_copy(t, q):
+        return rcopy(opart.at[t, 1 - core, q], osib.at[t, q], s_os.at[t, q], r_os.at[t, q], sib)
 
     def op_step(t, _):
         def op_half(h, _):
@@ -169,37 +234,32 @@
                 smat[...], rt, preferred_element_type=F32).astype(BF16).reshape(2, 8, TILE, 256)
             return 0
         lax.fori_loop(0, 4, op_half, 0)
-        os_copy(t).start()
+
+        def os_start(q, _):
+            os_copy(t, q).start()
+            return 0
+        lax.fori_loop(0, 8, os_start, 0)
         return 0
 
     lax.fori_loop(0, 4, op_step, 0)
 
-    cp_own_t.wait()
-
-    def t1_wait(i, _):
-        p = orb_peer(i)
-        rcopy(th.at[c], tbuf.at[j, p], s_t1.at[i], r_t1.at[p], (c, p)).wait_recv()
-        return 0
-
-    lax.fori_loop(1, 16, t1_wait, 0)
-    jx = (1 - xl) * 4 + y
-    cp_tx = rcopy(tbuf.at[j], tbuf.at[j], s_tx, r_tx, xpart)
-    cp_tx.start()
-
-    def ty(slot, which, up):
-        to = yp if up else ym
-        return rcopy(tbuf.at[slot], tbuf.at[slot], s_ty.at[which, int(up)], r_ty.at[which, int(up)],
-                     plane(xl * 4 + to))
-
-    ty(j, 0, True).start()
-    ty(j, 0, False).start()
+    def ty_start(g, _):
+        tx(jx, g).wait_recv()
+        ty(jx, 1, True, g).start()
+        ty(jx, 1, False, g).start()
+        return 0
+
+    lax.fori_loop(0, 4, ty_start, 0)
 
     def op_copy(t, i):
         jj = plane_peer(i)
         return rcopy(osum.at[t, jj], opl.at[t, j], s_op.at[t, i], r_op.at[t, j], plane(jj))
 
     def sum_step(t, _):
-        os_copy(t).wait_recv()
+        def os_wait(q, _):
+            os_copy(t, q).wait_recv()
+            return 0
+        lax.fori_loop(0, 8, os_wait, 0)
         osum[t] = (opart[t, core].astype(F32) + osib[t].astype(F32)).astype(BF16)
         opl[t, j] = osum[t, j]
 
@@ -210,10 +270,23 @@
         return 0
 
     lax.fori_loop(0, 4, sum_step, 0)
-
-    rcopy(tbuf.at[jx], tbuf.at[jx], s_tx, r_tx, xpart).wait_recv()
-    ty(jx, 1, True).start()
-    ty(jx, 1, False).start()
+    def tf_slot(which, up):
+        return (xl if which == 0 else 1 - xl) * 4 + (ym if up else yp)
+
+    def tf(which, up, g):
+        piece = tbuf.at[tf_slot(which, up), pl.ds(4 * g + (0 if up else 8), 4)]
+        return rcopy(piece, piece, s_tf.at[which, int(up), g], r_tf.at[which, int(up), g],
+                     plane(xl * 4 + (yp if up else ym)))
+
+    def tf_step(which):
+        def step(g, _):
+            for up in (True, False):
+                ty(tf_slot(which, up), which, up, g + (0 if up else 2)).wait_recv()
+                tf(which, up, g).start()
+            return 0
+        lax.fori_loop(0, 2, step, 0)
+
+    tf_step(0)
 
     od_copy = lambda t: rcopy(ored.at[t], obuf.at[o, t], s_od.at[t], r_od.at[o, t], (c, dest))
 
@@ -239,19 +312,7 @@
 
     lax.fori_loop(0, 4, red_step, 0)
 
-    def tf(which, up):
-        source = ym if up else yp
-        slot = (xl if which == 0 else 1 - xl) * 4 + source
-        h = 0 if up else 8
-        to = yp if up else ym
-        piece = tbuf.at[slot, pl.ds(h, 8)]
-        return rcopy(piece, piece, s_tf.at[which, int(up)], r_tf.at[which, int(up)], plane(xl * 4 + to))
-
-    for which in (0, 1):
-        for up in (True, False):
-            slot = (xl if which == 0 else 1 - xl) * 4 + (ym if up else yp)
-            rcopy(tbuf.at[slot], tbuf.at[slot], s_ty.at[which, int(up)], r_ty.at[which, int(up)], sib).wait_recv()
-            tf(which, up).start()
+    tf_step(1)
 
     def as_copy(p):
         return rcopy(abuf.at[core, p], abuf.at[core, p], s_as.at[p], r_as.at[p], sib)
@@ -261,11 +322,48 @@
 
     def a_fwd(i, _):
         p = lax.rem(o - i + 16, 16)
-        rcopy(cr.at[pl.ds(4 * p, 4)], abuf.at[core, p], s_a.at[i], r_a.at[p], (c, p)).wait_recv()
+        rcopy(pk.at[p], abuf.at[core, p], s_a.at[i], r_a.at[p], (c, p)).wait_recv()
         as_copy(p).start()
         return 0
 
     lax.fori_loop(1, 16, a_fwd, 0)
+
+    def as_wait(p, _):
+        rcopy(abuf.at[1 - core, p], abuf.at[1 - core, p], s_as.at[p], r_as.at[p], sib).wait_recv()
+        return 0
+
+    lax.fori_loop(0, 16, as_wait, 0)
+
+    def tr_step(i, _):
+        cols = pl.ds(pl.multiple_of(128 * i, 128), 128)
+        for k in range(2):
+            blk = abuf[k, pl.ds(2 * i, 2)].reshape(128, 896)
+            a_t[k, :, cols] = blk.T[:800]
+        return 0
+
+    lax.fori_loop(0, 8, tr_step, 0)
+    x_lo[...] = jnp.zeros_like(x_lo)
+    x_up[...] = jnp.zeros_like(x_up)
+    eye = iota((200, 200), 0) == iota((200, 200), 1)
+
+    def w_step(r, tot):
+        q = r // 2
+        jj = lax.rem(xl + r, 2) * 4 + lax.rem(y + q + (q // 2) * (5 - 2 * q), 4)
+        b = tbuf[jj].reshape(1024, 200)
+
+        def half(h, _):
+            x = jnp.dot(a_t[h], b,
+                        preferred_element_type=F32).astype(BF16).reshape(4, 200, 200)
+            for q in range(4):
+                x_up[4 * h + q, :200, :] = x[q]
+                x_lo[:, pl.ds(pl.multiple_of(1024 * h, 256) + 256 * q, 200)] = x[q]
+            return 0
+        lax.fori_loop(0, 2, half, 0)
+        d = jnp.dot(x_lo[...], x_up[...].reshape(2048, 200), preferred_element_type=F32)
+        value = jnp.sum(jnp.where(eye, d, 0.0))
+        return tot + jnp.where(iota((8, 128), 1) == 2 * jj + core, value, 0.0)
+
+    pairs = lax.fori_loop(0, 2, w_step, jnp.zeros((8, 128), F32))
 
     @pl.when(o == dest)
     def _():
@@ -303,45 +401,27 @@
             return 0
         lax.fori_loop(1, 16, send, 0)
 
-    for up in (True, False):
+    def ty_rest(g, _):
         for which in (0, 1):
-            slot = (xl if which == 0 else 1 - xl) * 4 + y2
-            piece = tbuf.at[slot, pl.ds(0 if up else 8, 8)]
-            rcopy(piece, piece, s_tf.at[which, int(up)], r_tf.at[which, int(up)], sib).wait_recv()
-
-    def as_wait(p, _):
-        rcopy(abuf.at[1 - core, p], abuf.at[1 - core, p], s_as.at[p], r_as.at[p], sib).wait_recv()
-        return 0
-
-    lax.fori_loop(0, 16, as_wait, 0)
-
-    def tr_step(i, _):
-        for h in range(8):
-            blk = abuf[i // 4, pl.ds(2 * h, 2), lax.rem(i, 4)].reshape(128, 200)
-            a_t[i, :, 128 * h:128 * h + 128] = blk.T
-        return 0
-
-    lax.fori_loop(0, 8, tr_step, 0)
-    eye = iota((200, 200), 0) == iota((200, 200), 1)
-
-    def w_step(jj, tot):
-        b = tbuf[jj].reshape(1024, 200)
-
-        def half(h, _):
-            x_buf[pl.ds(4 * h, 4)] = jnp.dot(
-                a_t[pl.ds(4 * h, 4)].reshape(800, 1024), b,
-                preferred_element_type=F32).astype(BF16).reshape(4, 200, 200)
-            return 0
-        lax.fori_loop(0, 2, half, 0)
-
-        def sq(i, d):
-            xb = x_buf[i]
-            return d + jnp.dot(xb, xb, preferred_element_type=F32)
-        d = lax.fori_loop(0, 8, sq, jnp.zeros((200, 200), F32))
-        value = jnp.sum(jnp.where(eye, d, 0.0))
-        return tot + jnp.where(iota((8, 128), 1) == 2 * jj + core, value, 0.0)
-
-    pairs = lax.fori_loop(0, 8, w_step, jnp.zeros((8, 128), F32))
+            for up in (True, False):
+                ty(tf_slot(which, up), which, up, g + (2 if up else 0)).wait_recv()
+        return 0
+
+    lax.fori_loop(0, 2, ty_rest, 0)
+
+    pairs = lax.fori_loop(2, 6, w_step, pairs)
+
+    def tf_wait(g, _):
+        for which in (0, 1):
+            for up in (True, False):
+                slot = (xl if which == 0 else 1 - xl) * 4 + y2
+                piece = tbuf.at[slot, pl.ds(4 * g + (0 if up else 8), 4)]
+                rcopy(piece, piece, s_tf.at[which, int(up), g], r_tf.at[which, int(up), g], sib).wait_recv()
+        return 0
+
+    lax.fori_loop(0, 2, tf_wait, 0)
+
+    pairs = lax.fori_loop(6, 8, w_step, pairs)
 
     ebuf[o] = pairs
 
@@ -391,10 +471,9 @@
         return 0
 
     lax.fori_loop(1, 16, e2_wait, 0)
-    en[...] = one_row + 0.5 / VECTORS * jnp.sum(e2buf[...], axis=0)
+    en[...] = (one_row + 0.5 / VECTORS * jnp.sum(e2buf[...], axis=0))[0, :16]
 
     def sent(i, _):
-        t1(i).wait_send()
         a2a(i).wait_send()
         fb_copy(i).wait_send()
         e1(i).wait_send()
@@ -403,19 +482,45 @@
 
     lax.fori_loop(1, 16, sent, 0)
 
+    def sent_t1(i, _):
+        t1(i).wait_send()
+        return 0
+
+    lax.fori_loop(1, 8, sent_t1, 0)
+
+    def sent_t1x(i, _):
+        t1x(z_peer(i)).wait_send()
+        return 0
+
+    lax.fori_loop(0, 8, sent_t1x, 0)
+
     def sent_as(p, _):
         as_copy(p).wait_send()
         return 0
 
     lax.fori_loop(0, 16, sent_as, 0)
-    cp_tx.wait_send()
-    for which in (0, 1):
+    def sent_th(g, _):
+        tx(j, g).wait_send()
         for up in (True, False):
-            ty(j if which == 0 else jx, which, up).wait_send()
-            tf(which, up).wait_send()
+            ty(j, 0, up, g).wait_send()
+            ty(jx, 1, up, g).wait_send()
+        return 0
+
+    lax.fori_loop(0, 4, sent_th, 0)
+
+    def sent_tf(g, _):
+        for which in (0, 1):
+            for up in (True, False):
+                tf(which, up, g).wait_send()
+        return 0
+
+    lax.fori_loop(0, 2, sent_tf, 0)
 
     def sent_o(t, _):
-        os_copy(t).wait_send()
+        def so(q, _):
+            os_copy(t, q).wait_send()
+            return 0
+        lax.fori_loop(0, 8, so, 0)
 
         def go(i, _):
             op_copy(t, i).wait_send()
@@ -448,21 +553,23 @@
     vm = pl.BlockSpec(memory_space=pltpu.VMEM)
     hbm = pl.BlockSpec(memory_space=pl.ANY)
     dma = pltpu.SemaphoreType.DMA
-    sems = [(6,), (16,), (16,), (), (), (2, 2), (2, 2), (2, 2), (2, 2), (), (16,),
-            (16,), (16,), (16,), (16,), (16,), (16,), (4,), (4,), (4, 8), (4, 8), (4,), (16, 4),
+    sems = [(6,), (8,), (16,), (16,), (4,), (4,), (2, 2, 4), (2, 2, 4), (2, 2, 2), (2, 2, 2), (), (16,),
+            (16,), (16,), (16,), (16,), (16,), (16,), (4, 8), (4, 8), (4, 8), (4, 8), (4,), (16, 4),
             (16,), (), (16,), (16,), (16,), (16,)]
     wout, en = pl.pallas_call(
         kernel,
-        out_shape=(jax.ShapeDtypeStruct((64, 200), BF16), jax.ShapeDtypeStruct((8, 128), F32)),
+        out_shape=(jax.ShapeDtypeStruct((64, 200), BF16), jax.ShapeDtypeStruct((16,), F32)),
         in_specs=[hbm, hbm, hbm, hbm, vm, vm],
         out_specs=(vm, vm),
         scratch_shapes=[
             pltpu.VMEM((64, 64, 200), BF16),
             pltpu.VMEM((64, 64, 1024), BF16),
             pltpu.VMEM((16, 64, 200), BF16),
+            pltpu.VMEM((16, 4096), F32),
             pltpu.VMEM((8, 16, 64, 200), BF16),
-            pltpu.VMEM((2, 16, 4, 64, 200), BF16),
-            pltpu.VMEM((8, 200, 1024), BF16),
+            pltpu.VMEM((16, 64, 896), BF16),
+            pltpu.VMEM((2, 16, 64, 896), BF16),
+            pltpu.VMEM((2, 800, 1024), BF16),
             pltpu.VMEM((16, 16, 128), F32),
             pltpu.VMEM((256, 1024), BF16),
             pltpu.VMEM((4, 2, 8, TILE, 1024), BF16),
@@ -476,7 +583,8 @@
             pltpu.VMEM((1024, 200), F32),
             pltpu.VMEM((16, 64, 200), BF16),
             pltpu.VMEM((64, 200), BF16),
-            pltpu.VMEM((8, 200, 200), BF16),
+            pltpu.VMEM((8, 256, 200), BF16),
+            pltpu.VMEM((200, 2048), BF16),
             pltpu.VMEM((16, 8, 128), F32),
             pltpu.VMEM((16, 8, 128), F32),
         ] + [dma(s) if s else dma for s in sems],
@@ -491,7 +599,7 @@
         flip(hcore_rotated),
         aux_fields,
     )
-    return flip(wout)[None], en[0, :16]
+    return flip(wout)[None], en
 
 
 def solution(mesh):

time: 145 us -> 119 us (0.82)
  Pallas kernels: 142 us -> 116 us
    pallas_call x1, Pallas kernels: 142 us -> 116 us  [body(): pl.pallas_call(kernel, out_shape=(jax.ShapeDtypeStruct((64, 200), BF16),...]
where the time goes in v2:
time: 119 us
  Pallas kernels  116 us (97%)
  local copies, waits for them, and re-layouts  2.55 us (2%)
    pallas_call x1, Pallas kernels, body(): pl.pallas_call(kernel, out_shape=(jax.ShapeDtypeStruct((64, 200), BF16),...  116 us
    unnamed x2, local copies, waits for them, and re-layouts  2.55 us

profile of v2, /device:TPU:1, one launch (start us, length us, event | category | flops | bytes accessed | tf_op | source)
XLA Modules:
  0.0 119.1 jit_solution(11804139424962639626)
XLA Ops:
  0.6 115.9 %shard_map.77 = (bf16[64,200]{1,0:T(8,128)(2,1)}, f32[16]{0:T(128)}) custom-call(bf16[64,200]{1,0:T(8,128)(2,1)} %bitcast.12, bf16[16,64,200]{2,1,0:T(8,128)(2,1)} %bitcast.11, bf16[64,64,1024]{2,1,0:T(8,128)(2,1)} %cv.1, bf16[64,64,200]{2,1,0:T(8,128)(2,1)} %bitcast.10, bf16[64,200]{1,0:T(8,128)(2,1)} %bitcast.13, f32[16,64]{1,0:T(8,128)} %aux.1), custom_call_target="tpu_custom_call" | custom-call | flops 14000000000 | bytes 12000000 | tf_op jit(solution)/shard_map/pallas_call | solution.py:559
  116.5 1.4 %copy.10 = bf16[1,200,64]{1,2,0:T(8,128)(2,1)} copy(bf16[1,200,64]{1,2,0:T(8,128)(2,1)} %bitcast.9) | data formatting | bytes 51200
  117.9 1.2 copy.11

commit v3 on v2

--- a/solution.py
+++ b/solution.py
@@ -365,6 +365,16 @@
 
     pairs = lax.fori_loop(0, 2, w_step, jnp.zeros((8, 128), F32))
 
+    def ty_rest(g, _):
+        for which in (0, 1):
+            for up in (True, False):
+                ty(tf_slot(which, up), which, up, g + (2 if up else 0)).wait_recv()
+        return 0
+
+    lax.fori_loop(0, 2, ty_rest, 0)
+
+    pairs = lax.fori_loop(2, 6, w_step, pairs)
+
     @pl.when(o == dest)
     def _():
         cp_phi_own.wait()
@@ -385,14 +395,14 @@
             src, dst = (degree - 1) % 2, degree % 2
 
             def mm(b, _):
-                rows = pl.ds(pl.multiple_of(b * 256, 256), 256)
-                lhs = obuf[pl.ds(4 * b, 4)].reshape(256, 1024)
+                rows = pl.ds(pl.multiple_of(b * 512, 512), 512)
+                lhs = obuf[pl.ds(8 * b, 8)].reshape(512, 1024)
                 prod = jnp.dot(lhs, term[src], preferred_element_type=F32)
-                new = (prod / degree).astype(BF16)
+                new = (prod * (1.0 / degree)).astype(BF16)
                 term[dst, rows] = new
                 acc[rows] = acc[rows] + new.astype(F32)
                 return 0
-            lax.fori_loop(0, 4, mm, 0)
+            lax.fori_loop(0, 2, mm, 0)
         res[...] = acc[...].astype(BF16).reshape(16, 64, 200)
 
         def send(i, _):
@@ -401,15 +411,6 @@
             return 0
         lax.fori_loop(1, 16, send, 0)
 
-    def ty_rest(g, _):
-        for which in (0, 1):
-            for up in (True, False):
-                ty(tf_slot(which, up), which, up, g + (2 if up else 0)).wait_recv()
-        return 0
-
-    lax.fori_loop(0, 2, ty_rest, 0)
-
-    pairs = lax.fori_loop(2, 6, w_step, pairs)
 
     def tf_wait(g, _):
         for which in (0, 1):

time: 119 us -> 117 us (0.983)
  Pallas kernels: 116 us -> 113 us
    pallas_call x1, Pallas kernels: 116 us -> 113 us  [body(): pl.pallas_call(kernel, out_shape=(jax.ShapeDtypeStruct((64, 200), BF16),...]
where the time goes in v3:
time: 117 us; the launch traced here: 116 us
  Pallas kernels  113 us (97%)
  local copies, waits for them, and re-layouts  2.55 us (2%)
    pallas_call x1, Pallas kernels, body(): pl.pallas_call(kernel, out_shape=(jax.ShapeDtypeStruct((64, 200), BF16),...  113 us
    unnamed x2, local copies, waits for them, and re-layouts  2.55 us

profile of v3, /device:TPU:1, one launch (start us, length us, event | category | flops | bytes accessed | tf_op | source)
XLA Modules:
  0.0 116.3 jit_solution(3254095305392435516)
XLA Ops:
  0.6 113.1 %shard_map.77 = (bf16[64,200]{1,0:T(8,128)(2,1)}, f32[16]{0:T(128)}) custom-call(bf16[64,200]{1,0:T(8,128)(2,1)} %bitcast.12, bf16[16,64,200]{2,1,0:T(8,128)(2,1)} %bitcast.11, bf16[64,64,1024]{2,1,0:T(8,128)(2,1)} %cv.1, bf16[64,64,200]{2,1,0:T(8,128)(2,1)} %bitcast.10, bf16[64,200]{1,0:T(8,128)(2,1)} %bitcast.13, f32[16,64]{1,0:T(8,128)} %aux.1), custom_call_target="tpu_custom_call" | custom-call | flops 14000000000 | bytes 12000000 | tf_op jit(solution)/shard_map/pallas_call | solution.py:560
  113.8 1.4 %copy.10 = bf16[1,200,64]{1,2,0:T(8,128)(2,1)} copy(bf16[1,200,64]{1,2,0:T(8,128)(2,1)} %bitcast.9) | data formatting | bytes 51200
  115.2 1.2 %copy.11 = f32[16]{0:T(128)} copy(f32[16]{0:T(128)} %get-tuple-element.9) | data formatting | bytes 128

commit v4 on v3

--- a/solution.py
+++ b/solution.py
@@ -288,30 +288,6 @@
 
     tf_step(0)
 
-    od_copy = lambda t: rcopy(ored.at[t], obuf.at[o, t], s_od.at[t], r_od.at[o, t], (c, dest))
-
-    def red_step(t, _):
-        def w(i, _):
-            jj = plane_peer(i)
-            rcopy(osum.at[t, jj], opl.at[t, jj], s_op.at[t, i], r_op.at[t, jj], plane(jj)).wait_recv()
-            return 0
-        lax.fori_loop(1, 8, w, 0)
-        tot = opl[t, 0].astype(F32)
-        for q in range(1, 8):
-            tot = tot + opl[t, q].astype(F32)
-
-        @pl.when(o != dest)
-        def _():
-            ored[t] = tot.astype(BF16)
-            od_copy(t).start()
-
-        @pl.when(o == dest)
-        def _():
-            obuf[o, t] = tot.astype(BF16)
-        return 0
-
-    lax.fori_loop(0, 4, red_step, 0)
-
     tf_step(1)
 
     def as_copy(p):
@@ -364,6 +340,30 @@
         return tot + jnp.where(iota((8, 128), 1) == 2 * jj + core, value, 0.0)
 
     pairs = lax.fori_loop(0, 2, w_step, jnp.zeros((8, 128), F32))
+
+    od_copy = lambda t: rcopy(ored.at[t], obuf.at[o, t], s_od.at[t], r_od.at[o, t], (c, dest))
+
+    def red_step(t, _):
+        def w(i, _):
+            jj = plane_peer(i)
+            rcopy(osum.at[t, jj], opl.at[t, jj], s_op.at[t, i], r_op.at[t, jj], plane(jj)).wait_recv()
+            return 0
+        lax.fori_loop(1, 8, w, 0)
+        tot = opl[t, 0].astype(F32)
+        for q in range(1, 8):
+            tot = tot + opl[t, q].astype(F32)
+
+        @pl.when(o != dest)
+        def _():
+            ored[t] = tot.astype(BF16)
+            od_copy(t).start()
+
+        @pl.when(o == dest)
+        def _():
+            obuf[o, t] = tot.astype(BF16)
+        return 0
+
+    lax.fori_loop(0, 4, red_step, 0)
 
     def ty_rest(g, _):
         for which in (0, 1):
@@ -433,7 +433,8 @@
         e1(i).start()
         return 0
 
-    lax.fori_loop(1, 16, e1_start, 0)
+    for i in range(1, 16):
+        e1_start(i, 0)
 
     def e1_wait(i, _):
         p = orb_peer(i)
@@ -449,7 +450,8 @@
         rcopy(land, land, s_w.at[0], r_w, (c, dest)).wait_recv()
         wout[...] = land[...]
 
-    lax.fori_loop(1, 16, e1_wait, 0)
+    for i in range(1, 16):
+        e1_wait(i, 0)
     bias = jnp.where(iota((16, 128), 1) < 64, fb_all, 0.0)
     coulomb = jnp.sum(bias * bias, axis=1, keepdims=True)
     wl = iota((16, 128), 0) == iota((16, 128), 1)
@@ -464,14 +466,16 @@
         e2(i).start()
         return 0
 
-    lax.fori_loop(1, 16, e2_start, 0)
+    for i in range(1, 16):
+        e2_start(i, 0)
 
     def e2_wait(i, _):
         p = lax.rem(c + i, 16)
         rcopy(e2buf.at[p], e2buf.at[p], s_e2.at[i], r_e2.at[p], (p, o)).wait_recv()
         return 0
 
-    lax.fori_loop(1, 16, e2_wait, 0)
+    for i in range(1, 16):
+        e2_wait(i, 0)
     en[...] = (one_row + 0.5 / VECTORS * jnp.sum(e2buf[...], axis=0))[0, :16]
 
     def sent(i, _):

time: 117 us -> 113 us (0.966)
  Pallas kernels: 113 us -> 110 us
    pallas_call x1, Pallas kernels: 113 us -> 110 us  [body(): pl.pallas_call(kernel, out_shape=(jax.ShapeDtypeStruct((64, 200), BF16),...]
where the time goes in v4:
time: 113 us
  Pallas kernels  110 us (97%)
  local copies, waits for them, and re-layouts  2.55 us (2%)
    pallas_call x1, Pallas kernels, body(): pl.pallas_call(kernel, out_shape=(jax.ShapeDtypeStruct((64, 200), BF16),...  110 us
    unnamed x2, local copies, waits for them, and re-layouts  2.55 us

profile of v4, /device:TPU:1, one launch (start us, length us, event | category | flops | bytes accessed | tf_op | source)
XLA Modules:
  0.0 112.8 jit_solution(11160539333756869098)
XLA Ops:
  0.6 109.6 %shard_map.77 = (bf16[64,200]{1,0:T(8,128)(2,1)}, f32[16]{0:T(128)}) custom-call(bf16[64,200]{1,0:T(8,128)(2,1)} %bitcast.12, bf16[16,64,200]{2,1,0:T(8,128)(2,1)} %bitcast.11, bf16[64,64,1024]{2,1,0:T(8,128)(2,1)} %cv.1, bf16[64,64,200]{2,1,0:T(8,128)(2,1)} %bitcast.10, bf16[64,200]{1,0:T(8,128)(2,1)} %bitcast.13, f32[16,64]{1,0:T(8,128)} %aux.1), custom_call_target="tpu_custom_call" | custom-call | flops 14000000000 | bytes 12000000 | tf_op jit(solution)/shard_map/pallas_call | solution.py:564
  110.3 1.4 %copy.10 = bf16[1,200,64]{1,2,0:T(8,128)(2,1)} copy(bf16[1,200,64]{1,2,0:T(8,128)(2,1)} %bitcast.9) | data formatting | bytes 51200
  111.7 1.2 %copy.11 = f32[16]{0:T(128)} copy(f32[16]{0:T(128)} %get-tuple-element.9) | data formatting | bytes 128

commit v5 on v4

--- a/solution.py
+++ b/solution.py
@@ -375,6 +375,30 @@
 
     pairs = lax.fori_loop(2, 6, w_step, pairs)
 
+    def tf_wait(g, _):
+        for which in (0, 1):
+            for up in (True, False):
+                slot = (xl if which == 0 else 1 - xl) * 4 + y2
+                piece = tbuf.at[slot, pl.ds(4 * g + (0 if up else 8), 4)]
+                rcopy(piece, piece, s_tf.at[which, int(up), g], r_tf.at[which, int(up), g], sib).wait_recv()
+        return 0
+
+    lax.fori_loop(0, 2, tf_wait, 0)
+
+    pairs = lax.fori_loop(6, 8, w_step, pairs)
+
+    ebuf[o] = pairs
+
+    def e1(i):
+        return rcopy(ebuf.at[o], ebuf.at[o], s_e1.at[i], r_e1.at[o], (c, orb_peer(i)))
+
+    def e1_start(i, _):
+        e1(i).start()
+        return 0
+
+    for i in range(1, 16):
+        e1_start(i, 0)
+
     @pl.when(o == dest)
     def _():
         cp_phi_own.wait()
@@ -412,43 +436,10 @@
         lax.fori_loop(1, 16, send, 0)
 
 
-    def tf_wait(g, _):
-        for which in (0, 1):
-            for up in (True, False):
-                slot = (xl if which == 0 else 1 - xl) * 4 + y2
-                piece = tbuf.at[slot, pl.ds(4 * g + (0 if up else 8), 4)]
-                rcopy(piece, piece, s_tf.at[which, int(up), g], r_tf.at[which, int(up), g], sib).wait_recv()
-        return 0
-
-    lax.fori_loop(0, 2, tf_wait, 0)
-
-    pairs = lax.fori_loop(6, 8, w_step, pairs)
-
-    ebuf[o] = pairs
-
-    def e1(i):
-        return rcopy(ebuf.at[o], ebuf.at[o], s_e1.at[i], r_e1.at[o], (c, orb_peer(i)))
-
-    def e1_start(i, _):
-        e1(i).start()
-        return 0
-
-    for i in range(1, 16):
-        e1_start(i, 0)
-
     def e1_wait(i, _):
         p = orb_peer(i)
         rcopy(ebuf.at[p], ebuf.at[p], s_e1.at[i], r_e1.at[p], (c, p)).wait_recv()
         return 0
-
-    @pl.when(o == dest)
-    def _():
-        wout[...] = res[o]
-
-    @pl.when(o != dest)
-    def _():
-        rcopy(land, land, s_w.at[0], r_w, (c, dest)).wait_recv()
-        wout[...] = land[...]
 
     for i in range(1, 16):
         e1_wait(i, 0)
@@ -477,6 +468,15 @@
     for i in range(1, 16):
         e2_wait(i, 0)
     en[...] = (one_row + 0.5 / VECTORS * jnp.sum(e2buf[...], axis=0))[0, :16]
+
+    @pl.when(o == dest)
+    def _():
+        wout[...] = res[o]
+
+    @pl.when(o != dest)
+    def _():
+        rcopy(land, land, s_w.at[0], r_w, (c, dest)).wait_recv()
+        wout[...] = land[...]
 
     def sent(i, _):
         a2a(i).wait_send()

time: 113 us -> 109 us (0.965)
  Pallas kernels: 110 us -> 106 us
    pallas_call x1, Pallas kernels: 110 us -> 106 us  [body(): pl.pallas_call(kernel, out_shape=(jax.ShapeDtypeStruct((64, 200), BF16),...]
where the time goes in v5:
time: 109 us
  Pallas kernels  106 us (97%)
  local copies, waits for them, and re-layouts  2.55 us (2%)
    pallas_call x1, Pallas kernels, body(): pl.pallas_call(kernel, out_shape=(jax.ShapeDtypeStruct((64, 200), BF16),...  106 us
    unnamed x2, local copies, waits for them, and re-layouts  2.55 us

profile of v5, /device:TPU:1, one launch (start us, length us, event | category | flops | bytes accessed | tf_op | source)
XLA Modules:
  0.0 108.8 jit_solution(15630254972831583481)
XLA Ops:
  0.6 105.6 %shard_map.77 = (bf16[64,200]{1,0:T(8,128)(2,1)}, f32[16]{0:T(128)}) custom-call(bf16[64,200]{1,0:T(8,128)(2,1)} %bitcast.12, bf16[16,64,200]{2,1,0:T(8,128)(2,1)} %bitcast.11, bf16[64,64,1024]{2,1,0:T(8,128)(2,1)} %cv.1, bf16[64,64,200]{2,1,0:T(8,128)(2,1)} %bitcast.10, bf16[64,200]{1,0:T(8,128)(2,1)} %bitcast.13, f32[16,64]{1,0:T(8,128)} %aux.1), custom_call_target="tpu_custom_call" | custom-call | flops 14000000000 | bytes 12000000 | tf_op jit(solution)/shard_map/pallas_call | solution.py:564
  106.3 1.4 %copy.10 = bf16[1,200,64]{1,2,0:T(8,128)(2,1)} copy(bf16[1,200,64]{1,2,0:T(8,128)(2,1)} %bitcast.9) | data formatting | bytes 51200
  107.6 1.2 %copy.11 = f32[16]{0:T(128)} copy(f32[16]{0:T(128)} %get-tuple-element.9) | data formatting | bytes 128
